TPU v7x, 256 devices: a whole 4x4x8 slice. The times are simulated.
256 devices in a mesh: group: 32 (over z, x), tensor: 8 (over y, core).
Axes of the slice: x: 4, y: 4, z: 8, core: 2. Of those that a mesh axis runs over, the one named last changes fastest.
Arguments:
- queries: bfloat16 [8192, 8192], P('group', 'tensor'), may hold values from -200 to 200
- rotated_keys: bfloat16 [8192, 1024], P('group', 'tensor'), may hold values from -8 to 8
- value_rows_all: bfloat16 [8192, 1024], P('group', 'tensor'), may hold values from -6 to 6
- output_weight: bfloat16 [8192, 8192], P('tensor', 'group'), may hold values from -0.0625 to 0.0625
- adapter_down: bfloat16 [32, 8192, 64], P('group', 'tensor'), may hold values from -0.0625 to 0.0625
- adapter_up: bfloat16 [32, 64, 8192], P(None, None, 'tensor'), may hold values from -0.75 to 0.75
- tenant_of_block: int32 [64], P('group'), may hold values from 0 to 31
- tenant_page_slots: int32 [32], replicated, may hold values from 0 to 31, each once
- prefix_length: int32 [32], replicated, may hold values from 1 to 256
Outputs:
- mixed: bfloat16 [8192, 8192], P('group', 'tensor')
Inputs may be any that keep to these rules, and one draw needn't show every extreme that they name: `tenant_page_slots`: each page slot is used by exactly one tenant.
All inputs are finite; a program needn't handle non-finite values.
Results may differ from a plain program's by a relative error of at most 0.023.
Values may be sent and summed in bfloat16 or wider, within the bound.
A program may use at most 128 MiB of HBM per device.

v0:
```python
import jax
import jax.numpy as jnp
from jax import lax
from jax.sharding import PartitionSpec as P

HEADS = 64
KV_HEADS = 8
HEAD_DIM = 128
BLOCK_SIZE = 128


def layout(tenants, prefix_length):
    blocks = tenants.shape[0]
    tenant_count = prefix_length.shape[0]
    block_index = jnp.arange(blocks)
    same_tenant = tenants[:, None] == tenants[None, :]
    earlier = jnp.sum(
        (same_tenant & (block_index[None, :] < block_index[:, None])).astype(jnp.int32), axis=1
    )
    row_tenant = jnp.repeat(tenants, BLOCK_SIZE)
    position = jnp.repeat(earlier, BLOCK_SIZE) * BLOCK_SIZE + jnp.tile(
        jnp.arange(BLOCK_SIZE), blocks
    )
    matches = row_tenant[:, None] == jnp.arange(tenant_count)[None, :]
    length = jnp.sum(jnp.where(matches, prefix_length[None, :], 0), axis=1)
    row_validity = position < length
    row_index = jnp.arange(blocks * BLOCK_SIZE)
    visible = (
        (row_tenant[:, None] == row_tenant[None, :])
        & (row_index[None, :] <= row_index[:, None])
        & row_validity[None, :]
    )
    return (visible, row_validity)


def per_device(
    queries,
    rotated_keys,
    value_rows_all,
    output_weight,
    adapter_down,
    adapter_up,
    tenant_of_block,
    tenant_page_slots,
    prefix_length,
):
    block_count = queries.shape[0]
    local_width = queries.shape[1]
    groups = HEADS // KV_HEADS
    kv_local = rotated_keys.shape[1] // HEAD_DIM
    blocks = tenant_of_block.shape[0]
    tenant_count = tenant_page_slots.shape[0]
    visible, row_validity = layout(tenant_of_block, prefix_length)
    query_heads = queries.reshape(block_count, kv_local, groups, HEAD_DIM)
    key_heads = rotated_keys.reshape(block_count, kv_local, HEAD_DIM)
    value_heads = value_rows_all.reshape(block_count, kv_local, HEAD_DIM)
    scores = jnp.einsum(
        "rkgd,skd->kgrs", query_heads, key_heads, preferred_element_type=jnp.float32
    ) * HEAD_DIM ** (-0.5)
    scores = jnp.where(visible[None, None], scores, -jnp.inf)
    peak = jnp.max(scores, axis=-1, keepdims=True)
    expo = jnp.exp(scores - peak)
    probs = (expo / jnp.sum(expo, axis=-1, keepdims=True)).astype(jnp.bfloat16)
    head_result = jnp.einsum(
        "kgrs,skd->rkgd", probs, value_heads, preferred_element_type=jnp.float32
    )
    head_result = head_result.reshape(block_count, local_width).astype(jnp.bfloat16)
    onehot = tenant_of_block[:, None] == jnp.arange(tenant_count)[None, :]
    page_slots = jnp.sum(jnp.where(onehot, tenant_page_slots[None, :], 0), axis=1)
    page_selector = (page_slots[:, None] == jnp.arange(tenant_count)[None, :]).astype(jnp.bfloat16)
    rows_per_block = head_result.reshape(blocks, BLOCK_SIZE, local_width)
    block_piece = lax.all_gather(adapter_down, "group", axis=0, tiled=True)
    slots = jnp.arange(block_piece.shape[0])
    chosen = (page_slots[:, None] == slots[None, :]).astype(jnp.bfloat16)
    picked = jnp.einsum(
        "bj,jir->bir", chosen, block_piece, preferred_element_type=jnp.float32
    ).astype(jnp.bfloat16)
    shrunk_part = jnp.einsum(
        "bsi,bir->bsr", rows_per_block, picked, preferred_element_type=jnp.float32
    )
    down_projected = lax.psum(shrunk_part.astype(jnp.bfloat16), "tensor")
    up_pages = jnp.einsum(
        "jf,fsq->jsq", page_selector, adapter_up, preferred_element_type=jnp.float32
    ).astype(jnp.bfloat16)
    adapter_output = jnp.einsum(
        "bsr,brc->bsc", down_projected, up_pages, preferred_element_type=jnp.float32
    ).reshape(block_count, adapter_up.shape[2])
    projected = jnp.dot(
        lax.all_gather(head_result, "group", axis=0, tiled=True),
        output_weight,
        preferred_element_type=jnp.float32,
    ).astype(jnp.bfloat16)
    partial_value = lax.all_to_all(
        projected, "group", split_axis=0, concat_axis=1, tiled=True
    ).astype(jnp.float32)
    base_output = lax.psum_scatter(
        partial_value.astype(jnp.bfloat16), "tensor", scatter_dimension=1, tiled=True
    ).astype(jnp.float32)
    return jnp.where(row_validity[:, None], base_output + adapter_output, 0.0).astype(jnp.bfloat16)


def solution(mesh):
    placed = (
        P("group", "tensor"),
        P("group", "tensor"),
        P("group", "tensor"),
        P("tensor", "group"),
        P("group", "tensor", None),
        P(None, None, "tensor"),
        P("group"),
        P(),
        P(),
    )
    return jax.shard_map(
        per_device, mesh=mesh, in_specs=placed, out_specs=P("group", "tensor"), check_vma=False
    )
```

profile of v0, /device:TPU:121, one launch (start us, length us, event | category | flops | bytes accessed | tf_op | source)
XLA Modules:
  0.0 348.9 jit_solution(1154075169617286358)
XLA Ops:
  6.5 0.0 copy-start
  6.5 0.0 copy-start.2
  6.5 0.0 all-gather.3.cloned.1.call-start
  6.5 0.9 fusion.26
  7.5 0.7 broadcast_bitcast_fusion
  8.2 0.7 select_reduce_fusion
  8.9 0.1 bitcast_compare_fusion
  9.0 0.1 fusion.21
  9.2 1.5 fusion.30
  10.7 0.3 fusion.4
  11.0 0.0 copy-done.2
  11.0 1.3 convolution_convert_fusion.1
  12.3 0.0 all-gather.3.cloned.1.call-update
  12.4 147.9 %all-gather.3.cloned.1.call-done = bf16[8192,1024]{0,1:T(8,128)(2,1)} async-done(((bf16[256,1024]{0,1:T(8,128)(2,1)}), bf16[8192,1024]{0,1:T(8,128)(2,1)}) %all-gather.3.cloned.1.call-update) | async-done | bytes 16777232 | tf_op jit(solution)/shard_map/all_gather | solution.py:89
  160.2 0.0 copy-done
  160.2 12.5 %convolution_convert_fusion = bf16[8192,256]{1,0:T(8,128)(2,1)} fusion(bf16[8192,1024]{0,1:T(8,128)(2,1)} %all-gather.3.cloned.1.call-done, bf16[1024,256]{1,0:T(8,128)(2,1)S(1)} %copy-done), kind=kOutput, calls=%fused_computation | convolution fusion | flops 4297064448 | bytes 21495808 | tf_op jit(solution)/shard_map/dot_general | solution.py:88
  172.7 6.6 %all-to-all-start = ((bf16[32,256,256]{2,1,0:T(8,128)(2,1)}), bf16[32,256,256]{2,1,0:T(8,128)(2,1)}, u32[]{:S(2)}, u32[]{:S(2)}) async-start(bf16[32,256,256]{2,1,0:T(8,128)(2,1)} %bitcast.58), calls=%async_computation | async-start | bytes 8388608 | tf_op jit(solution)/shard_map/all_to_all | solution.py:93
  179.3 0.0 all-gather.5.cloned.1.call-start
  179.4 0.7 all-gather.5.cloned.1.call-update
  180.1 0.2 reduce-scatter.2.cloned.1.call-start
  180.3 102.0 %all-to-all-done = bf16[32,256,256]{2,1,0:T(8,128)(2,1)} async-done(((bf16[32,256,256]{2,1,0:T(8,128)(2,1)}), bf16[32,256,256]{2,1,0:T(8,128)(2,1)}, u32[]{:S(2)}, u32[]{:S(2)}) %all-to-all-start) | async-done | bytes 4194336 | tf_op jit(solution)/shard_map/all_to_all | solution.py:93
  282.3 4.7 %copy.31 = bf16[32,32,8,256]{3,2,0,1:T(8,128)(2,1)} copy(bf16[32,32,8,256]{3,2,1,0:T(8,128)(2,1)} %bitcast.21) | data formatting | bytes 8388608 | tf_op jit(solution)/shard_map/all_to_all | solution.py:93
  287.0 0.0 copy-start.1
  287.0 0.0 copy-start.3
  287.0 0.0 copy-start.4
  287.0 0.0 reduce-scatter.2.cloned.1.call-update
  287.0 1.0 copy-done.1
  288.1 0.1 convert_element_type.59
  288.2 0.0 copy-done.3
  288.2 0.0 copy-done.4
  288.2 0.2 fusion.27
  288.4 6.8 %fusion.8 = bf16[2,64,1024]{2,0,1:T(2,128)(2,1)S(1)} fusion(bf16[32,64,1024]{2,1,0:T(8,128)(2,1)} %param.14, s32[2]{0:T(128)S(1)} %fusion.27), kind=kOutput, calls=%fused_computation.11 | convolution fusion | flops 8519744 | bytes 4456456 | tf_op jit(solution)/shard_map/jf,fsq->jsq/dot_general | solution.py:82
  295.2 2.7 all-gather.5.cloned.1.call-done
  297.9 6.8 %fusion.5 = bf16[2,1024,64]{1,0,2:T(2,128)(2,1)S(1)} fusion(bf16[32,1024,64]{1,2,0:T(8,128)(2,1)} %all-gather.5.cloned.1.call-done, s32[2]{0:T(128)S(1)} %fusion.27), kind=kOutput, calls=%fused_computation.10 | convolution fusion | flops 8519744 | bytes 4456456 | tf_op jit(solution)/shard_map/bj,jir->bir/dot_general | solution.py:75
  304.7 0.2 convolution_convert_fusion.2
  305.0 28.4 %psum.7 = bf16[2,128,64]{1,2,0:T(8,128)(2,1)S(1)} all-reduce(bf16[2,128,64]{1,2,0:T(8,128)(2,1)S(1)} %convolution_convert_fusion.2), channel_id=1, replica_groups=mesh['group'=32,'tensor'=8] {'tensor'}, use_global_device_ids=true, to_apply=%region_6.7 | all-reduce | flops 16384 | bytes 65536 | tf_op jit(solution)/shard_map/psum | solution.py:81
  333.3 0.3 fusion.17
  333.7 6.5 %reduce-scatter.2.cloned.1.call-done = bf16[256,1024]{1,0:T(8,128)(2,1)} async-done(((bf16[256,8192]{1,0:T(8,128)(2,1)}), bf16[256,1024]{1,0:T(8,128)(2,1)}) %reduce-scatter.2.cloned.1.call-update) | async-done | bytes 524304 | tf_op jit(solution)/shard_map/reduce_scatter | solution.py:96
  340.2 2.2 fusion.12
  (1 shorter events, 0.0 us)
Async XLA Ops:
  6.5 153.7 %copy-start = (bf16[1024,256]{1,0:T(8,128)(2,1)S(1)}, bf16[1024,256]{1,0:T(8,128)(2,1)}, u32[]{:S(2)}) copy-start(bf16[1024,256]{1,0:T(8,128)(2,1)} %param.12) | copy-start | bytes 1572868
  6.5 4.5 %copy-start.2 = (bf16[256,128]{1,0:T(8,128)(2,1)S(1)}, bf16[256,128]{1,0:T(8,128)(2,1)}, u32[]{:S(2)}) copy-start(bf16[256,128]{1,0:T(8,128)(2,1)} %param.11) | copy-start | bytes 196612
  6.5 153.7 %all-gather.3.cloned.1.call-start = ((), (), s32[]{:S(2)}) async-start(), calls=%async_computation.2 | async-start | bytes 17301504 | tf_op jit(solution)/shard_map/all_gather | solution.py:89
  172.7 109.6 %all-to-all-start = ((bf16[32,256,256]{2,1,0:T(8,128)(2,1)}), bf16[32,256,256]{2,1,0:T(8,128)(2,1)}, u32[]{:S(2)}, u32[]{:S(2)}) async-start(bf16[32,256,256]{2,1,0:T(8,128)(2,1)} %bitcast.58), calls=%async_computation | async-start | bytes 8388608 | tf_op jit(solution)/shard_map/all_to_all | solution.py:93
  179.3 118.6 %all-gather.5.cloned.1.call-start = ((), (), s32[]{:S(2)}) async-start(), calls=%async_computation.4 | async-start | bytes 4325376 | tf_op jit(solution)/shard_map/all_gather | solution.py:72
  180.1 160.1 %reduce-scatter.2.cloned.1.call-start = ((), (), s32[]{:S(2)}) async-start(), calls=%async_computation.3 | async-start | bytes 4718592 | tf_op jit(solution)/shard_map/reduce_scatter | solution.py:96
  287.0 1.0 copy-start.1
  287.0 1.2 copy-start.3
  287.0 1.2 copy-start.4
Sparse Core Ops, SparseCore 0:
  12.5 147.7 all-gather.2
  182.8 115.1 all-gather.4
  300.5 39.6 reduce-scatter.1
where the time goes:
time: 352 us; the launch traced here: 349 us
  waiting for transfers between devices  260 us (74%)
  matrix products  29.5 us (8%)
  blocking collectives  28.4 us (8%)
  between operations  13.2 us (4%)
  starting transfers between devices  6.85 us (2%)
  local copies, waits for them, and re-layouts  6.58 us (2%)
  other arithmetic  4.53 us (1%)
    all_gather x1, waiting for transfers between devices, per_device(): lax.all_gather(head_result, 'group', axis=0, tiled=True)  148 us
    all_to_all x1, waiting for transfers between devices, per_device(): lax.all_to_all(projected, 'group', split_axis=0, concat_axis=1, tiled=True)  102 us
    psum x1, blocking collectives, per_device(): down_projected = lax.psum(shrunk_part.astype(jnp.bfloat16), 'tensor')  28.4 us
    dot_general x1, matrix products, per_device(): jnp.dot(lax.all_gather(head_result, 'group', axis=0, tiled=True), output_...  12.5 us
  transfers between devices with their start and end apart: 4, of which 4 were waited for; matrix products, arithmetic and copies ran while one was open for 5% of the time, Pallas kernels for 0%

commit v1 on v0

v1 whole, which is shorter than its diff:
```python
import functools

import jax
import jax.numpy as jnp
from jax import lax
from jax.experimental import pallas as pl
from jax.experimental.pallas import tpu as pltpu
from jax.sharding import PartitionSpec as P

MESH = pl.DeviceIdType.MESH
HEADS = 8
DIM = 128
BLOCK = 128
NZ, NX, NY, NT = 8, 4, 4, 8
WIDTH = 1024
STEPS = 8
LAST = 7
EXP2_SCALE = DIM ** (-0.5) * 1.4426950408889634
F32 = jnp.float32
BF16 = jnp.bfloat16


def matmul(a, b):
    return jnp.dot(a, b, preferred_element_type=F32)


def matmul_t(a, b):
    return lax.dot_general(a, b, (((1,), (1,)), ((), ())), preferred_element_type=F32)


def kernel(
    q_hbm, k_hbm, v_hbm, w_hbm, down_hbm, up_hbm, tenant_ref, slot_ref, length_ref,
    out_ref,
    qv, kv, vv, hbuf, slots, wbuf, pbuf, upv,
    psend, prec, own, rsend, rrec, fsend, fin, acc,
    asend, arec, tsend, trec,
    lsem, wss, wrs, pss, prs, hss, hrs, sss, srs, pxs, pxr, rss, rrs, fss, frs,
    axs, axr, ats, atr,
):
    g, t = lax.axis_index("group"), lax.axis_index("tensor")
    z, x = g // NX, g % NX
    y, c = t // 2, t % 2
    z_next = ((z + 1) % NZ) * NX + x
    z_prev = ((z + NZ - 1) % NZ) * NX + x

    barrier = pltpu.get_barrier_semaphore()
    for peer in (z_next, z_prev):
        pl.semaphore_signal(barrier, inc=1, device_id=(peer, t), device_id_type=MESH)

    def greet(d, carry):
        peer = (x * NT + t + d) % (NX * NT)
        pl.semaphore_signal(
            barrier, inc=1, device_id=(z * NX + peer // NT, peer % NT), device_id_type=MESH
        )
        return carry

    lax.fori_loop(1, NX * NT, greet, 0)
    pl.semaphore_wait(barrier, NX * NT + 1)

    def remote(src, dst, ssem, rsem, device):
        return pltpu.make_async_remote_copy(
            src_ref=src, dst_ref=dst, send_sem=ssem, recv_sem=rsem,
            device_id=device, device_id_type=MESH,
        )

    def item(d, s):
        half = s % 2 if d == 0 else 1 - s % 2
        tile = (z + NZ - s // 2) % NZ if d == 0 else (z + s // 2) % NZ
        return tile, half

    def w_copy(d, s, first=False):
        tile, half = item(d, s)
        src = w_hbm.at[:, half * 128 : half * 128 + 128] if first else wbuf.at[tile, half]
        return remote(
            src, wbuf.at[tile, half], wss.at[d, s], wrs.at[d, s],
            (z_next if d == 0 else z_prev, t),
        )

    def p_copy(d, s, first=False):
        tile, half = item(d, s)
        src = down_hbm.at[half * 32 : half * 32 + 32, :] if first else pbuf.at[tile, half]
        return remote(
            src, pbuf.at[tile, half], pss.at[d, s], prs.at[d, s],
            (z_next if d == 0 else z_prev, t),
        )

    for make in (p_copy, w_copy):
        for s in range(2):
            for d in range(2):
                make(d, s, True).start()

    def arrived(make, j):
        for d in range(2):
            make(d, j - 1).wait_recv()
            if j + 1 < LAST:
                make(d, j + 1).start()

    q_in = pltpu.make_async_copy(q_hbm, qv, lsem.at[0])
    k_in = pltpu.make_async_copy(k_hbm, kv, lsem.at[1])
    v_in = pltpu.make_async_copy(v_hbm, vv, lsem.at[2])
    w_in = [
        pltpu.make_async_copy(w_hbm.at[:, h * 128 : h * 128 + 128], wbuf.at[z, h], lsem.at[3 + h])
        for h in range(2)
    ]
    d_in = [
        pltpu.make_async_copy(down_hbm.at[h * 32 : h * 32 + 32, :], pbuf.at[z, h], lsem.at[5 + h])
        for h in range(2)
    ]
    up_in = pltpu.make_async_copy(up_hbm, upv, lsem.at[7])
    local = [k_in, q_in, v_in] + w_in + d_in + [up_in]
    for copy in local:
        copy.start()

    tenant0, tenant1 = tenant_ref[0], tenant_ref[1]
    same = tenant0 == tenant1
    length0, length1 = length_ref[tenant0], length_ref[tenant1]
    slot0, slot1 = slot_ref[tenant0], slot_ref[tenant1]
    shift1 = jnp.where(same, BLOCK, 0)
    reach0 = jnp.where(same, length0, 0)

    rows8 = lax.broadcasted_iota(jnp.int32, (8, 128), 0)
    slots[x] = jnp.where(rows8 == 0, slot0, slot1).astype(F32)

    def slot_copy(d):
        return remote(
            slots.at[x], slots.at[x], sss.at[d - 1], srs.at[d - 1], (z * NX + (x + d) % NX, t)
        )

    for d in range(1, NX):
        slot_copy(d).start()

    def h_copy(d, i):
        if i < 2:
            b, tile = i, x
        else:
            b, tile = d, (x + NX - 1) % NX if d == 0 else (x + 1) % NX
        at = hbuf.at[b, pl.ds(pl.multiple_of(tile * BLOCK, BLOCK), BLOCK), :]
        to = (x + 1) % NX if d == 0 else (x + NX - 1) % NX
        return remote(at, at, hss.at[d, i], hrs.at[d, i], (z * NX + to, t))

    k_in.wait()
    q_in.wait()
    v_in.wait()
    row = lax.broadcasted_iota(jnp.int32, (BLOCK, BLOCK), 0)
    col = lax.broadcasted_iota(jnp.int32, (BLOCK, BLOCK), 1)
    causal = col <= row
    masks = (
        [causal & (col < length0)],
        [col < reach0, causal & (col + shift1 < length1)],
    )
    here = pl.ds(pl.multiple_of(x * BLOCK, BLOCK), BLOCK)
    for b in range(2):
        keys = [kv[j * BLOCK : (j + 1) * BLOCK, :] for j in range(b + 1)]
        values = [vv[j * BLOCK : (j + 1) * BLOCK, :] for j in range(b + 1)]
        for h in range(HEADS):
            query = qv[b * BLOCK : (b + 1) * BLOCK, h * DIM : (h + 1) * DIM]
            scores = [
                jnp.where(mask, matmul_t(query, key), -1e30)
                for mask, key in zip(masks[b], keys)
            ]
            peak = functools.reduce(
                jnp.maximum, [jnp.max(s, axis=1, keepdims=True) for s in scores]
            )
            expo = [jnp.exp2((s - peak) * EXP2_SCALE) for s in scores]
            total = functools.reduce(
                jnp.add, [jnp.sum(e, axis=1, keepdims=True) for e in expo]
            )
            inverse = 1.0 / total
            mixed = functools.reduce(
                jnp.add,
                [matmul((e * inverse).astype(BF16), value) for e, value in zip(expo, values)],
            )
            hbuf[b, here, h * DIM : (h + 1) * DIM] = mixed.astype(BF16)
        for d in range(2):
            h_copy(d, b).start()

    arrived(p_copy, 1)
    arrived(p_copy, 2)
    arrived(w_copy, 1)
    arrived(p_copy, 3)
    h_copy(0, 0).wait_recv()
    h_copy(0, 2).start()
    arrived(p_copy, 4)
    arrived(w_copy, 2)
    arrived(p_copy, 5)
    h_copy(1, 1).wait_recv()
    h_copy(1, 2).start()
    arrived(p_copy, 6)
    for d, i in ((0, 1), (1, 0), (0, 2), (1, 2)):
        h_copy(d, i).wait_recv()
    arrived(p_copy, 7)
    for copy in w_in + d_in + [up_in]:
        copy.wait()
    for d in range(1, NX):
        slot_copy(d).wait_recv()

    def tiles_of(k):
        off, half = (k + 1) // 2, (k + 1) % 2
        return ((z + NZ - off) % NZ, half), ((z + off) % NZ, 1 - half)

    def pair_copy(k):
        return remote(psend.at[k], prec.at[k], pxs.at[k], pxr.at[k], (g, 2 * y + 1 - c))

    def sum_copy(k, d):
        to = (y + d) % NY
        return remote(
            rsend.at[k, to], rrec.at[k, d - 1], rss.at[k, d - 1], rrs.at[k, d - 1], (g, 2 * to + c)
        )

    def fin_copy(k, i):
        tile, half = tiles_of(k)[i]
        return remote(
            fsend.at[k, i],
            fin.at[x, half, pl.ds(pl.multiple_of(c * BLOCK, BLOCK), BLOCK), :],
            fss.at[k, i], frs.at[x, half, c], (z * NX + y, tile),
        )

    def stays(tile):
        return (x == y) & (tile == t)

    def finish(k):
        part = rsend[k, y].astype(F32)
        for d in range(1, NY):
            sum_copy(k, d).wait_recv()
            part = part + rrec[k, d - 1].astype(F32)
        part = part.astype(BF16)
        for i, (tile, half) in enumerate(tiles_of(k)):
            piece = part[:, i * 128 : (i + 1) * 128]

            @pl.when(stays(tile))
            def _():
                fin[x, half, pl.ds(pl.multiple_of(c * BLOCK, BLOCK), BLOCK), :] = piece

            @pl.when(jnp.logical_not(stays(tile)))
            def _():
                fsend[k, i] = piece
                fin_copy(k, i).start()

    def shrink_copy(d):
        return remote(
            asend.at[(x + d) % NX], arec.at[d - 1], axs.at[d - 1], axr.at[d - 1],
            (z * NX + (x + d) % NX, t),
        )

    def tensor_copy(d):
        return remote(tsend, trec.at[d - 1], ats.at[d - 1], atr.at[d - 1], (g, (t + d) % NT))

    def shrink():
        pages = pbuf[...].reshape(NZ * 64, WIDTH)
        lane = lax.broadcasted_iota(jnp.int32, (1, NZ * 64), 1)
        page = ((lane // 64) * NX + x).astype(F32)
        at = lax.broadcasted_iota(jnp.int32, (NZ * 64, 128), 0) % 64
        to = lax.broadcasted_iota(jnp.int32, (NZ * 64, 128), 1)
        for i in range(NX):
            total = jnp.zeros((BLOCK, 128), F32)
            for b in range(2):
                rows = matmul_t(hbuf[b, i * BLOCK : (i + 1) * BLOCK, :], pages)
                slot = jnp.concatenate([slots[i, b : b + 1, :]] * (NZ * 64 // 128), axis=1)
                rows = jnp.where(slot == page, rows, 0.0).astype(BF16)
                total = total + matmul(rows, (to == at + 64 * b).astype(BF16))
            asend[i] = total.astype(BF16)
        for d in range(1, NX):
            shrink_copy(d).start()

    def shrink_x():
        total = asend[x].astype(F32)
        for d in range(1, NX):
            shrink_copy(d).wait_recv()
            total = total + arec[d - 1].astype(F32)
        tsend[...] = total.astype(BF16)
        for d in range(1, NT):
            tensor_copy(d).start()

    def expand():
        total = tsend[...].astype(F32)
        for d in range(1, NT):
            tensor_copy(d).wait_recv()
            total = total + trec[d - 1].astype(F32)
        shrunk = total.astype(BF16)
        lane = lax.broadcasted_iota(jnp.int32, (BLOCK, 128), 1)
        for b, slot in enumerate((slot0, slot1)):
            acc[b * BLOCK : (b + 1) * BLOCK, :] = matmul(
                jnp.where(lane // 64 == b, shrunk, jnp.zeros_like(shrunk)),
                jnp.concatenate([upv[slot], upv[slot]], axis=0),
            )

    def step(k, carry):
        @pl.when((k == 2) | (k >= 4))
        def _():
            j = jnp.where(k == 2, 3, k)
            for d in range(2):
                w_copy(d, j - 1).wait_recv()

            @pl.when(j + 1 < LAST)
            def _():
                for d in range(2):
                    w_copy(d, j + 1).start()

        (tile_r, half_r), (tile_l, half_l) = tiles_of(k)
        weights = jnp.concatenate([wbuf[tile_r, half_r], wbuf[tile_l, half_l]], axis=1)
        psend[k] = matmul(hbuf[1 - c], weights).astype(BF16)
        pair_copy(k).start()
        own[...] = matmul(hbuf[c], weights)

        @pl.when(k == 1)
        def _():
            shrink()

        @pl.when(k == 3)
        def _():
            shrink_x()

        @pl.when(k == 4)
        def _():
            expand()

        @pl.when(k > 0)
        def _():
            finish(k - 1)

        pair_copy(k).wait_recv()
        total = (own[...] + prec[k].astype(F32)).astype(BF16)
        for i in range(NY):
            rsend[k, i] = total[i * BLOCK : (i + 1) * BLOCK, :]
        for d in range(1, NY):
            sum_copy(k, d).start()
        return carry

    lax.fori_loop(0, STEPS, step, 0)
    finish(STEPS - 1)

    def sent(s, carry):
        for d in range(2):
            p_copy(d, s).wait_send()
            w_copy(d, s).wait_send()
        return carry

    lax.fori_loop(0, LAST, sent, 0)
    for d in range(2):
        for i in range(3):
            h_copy(d, i).wait_send()
    for d in range(1, NX):
        slot_copy(d).wait_send()
        shrink_copy(d).wait_send()
    for d in range(1, NT):
        tensor_copy(d).wait_send()

    def stepped(k, carry):
        pair_copy(k).wait_send()
        for d in range(1, NY):
            sum_copy(k, d).wait_send()
        for i, (tile, _) in enumerate(tiles_of(k)):

            @pl.when(jnp.logical_not(stays(tile)))
            def _():
                fin_copy(k, i).wait_send()

        return carry

    lax.fori_loop(0, STEPS, stepped, 0)

    for i in range(NX):
        for cc in range(2):
            mine = (x == i) & (t == 2 * x + cc)
            for half in range(2):

                @pl.when(jnp.logical_not(mine))
                def _():
                    at = fin.at[i, half, cc * BLOCK : (cc + 1) * BLOCK, :]
                    remote(at, at, fss.at[0, 0], frs.at[i, half, cc], (z_next, t)).wait_recv()

    position = lax.broadcasted_iota(jnp.int32, (BLOCK, 128), 0)
    valid = (position < length0, position + shift1 < length1)
    for b in range(2):
        for i in range(NX):
            for half in range(2):
                cols = slice(i * 256 + half * 128, i * 256 + half * 128 + 128)
                base = fin[i, half, b * BLOCK : (b + 1) * BLOCK, :].astype(F32)
                value = base + acc[b * BLOCK : (b + 1) * BLOCK, cols]
                out_ref[b * BLOCK : (b + 1) * BLOCK, cols] = jnp.where(
                    valid[b], value, 0.0
                ).astype(BF16)


def per_device(q, k, v, w, down, up, tenants, page_slots, lengths):
    dma = pltpu.SemaphoreType.DMA
    anywhere = pl.BlockSpec(memory_space=pl.ANY)
    scalars = pl.BlockSpec(memory_space=pltpu.SMEM)
    rows = 2 * BLOCK
    return pl.pallas_call(
        kernel,
        out_shape=jax.ShapeDtypeStruct((rows, WIDTH), BF16),
        in_specs=[anywhere] * 6 + [scalars] * 3,
        out_specs=pl.BlockSpec(memory_space=pltpu.VMEM),
        scratch_shapes=[
            pltpu.VMEM((rows, WIDTH), BF16),
            pltpu.VMEM((rows, DIM), BF16),
            pltpu.VMEM((rows, DIM), BF16),
            pltpu.VMEM((2, NX * BLOCK, WIDTH), BF16),
            pltpu.VMEM((NX, 8, 128), F32),
            pltpu.VMEM((NZ, 2, WIDTH, 128), BF16),
            pltpu.VMEM((NZ, 2, 32, WIDTH), BF16),
            pltpu.VMEM((32, 64, WIDTH), BF16),
            pltpu.VMEM((STEPS, NX * BLOCK, 256), BF16),
            pltpu.VMEM((STEPS, NX * BLOCK, 256), BF16),
            pltpu.VMEM((NX * BLOCK, 256), F32),
            pltpu.VMEM((STEPS, NY, BLOCK, 256), BF16),
            pltpu.VMEM((STEPS, NY - 1, BLOCK, 256), BF16),
            pltpu.VMEM((STEPS, 2, BLOCK, 128), BF16),
            pltpu.VMEM((NX, 2, rows, 128), BF16),
            pltpu.VMEM((rows, WIDTH), F32),
            pltpu.VMEM((NX, BLOCK, 128), BF16),
            pltpu.VMEM((NX - 1, BLOCK, 128), BF16),
            pltpu.VMEM((BLOCK, 128), BF16),
            pltpu.VMEM((NT - 1, BLOCK, 128), BF16),
            dma((8,)),
            dma((2, LAST)), dma((2, LAST)), dma((2, LAST)), dma((2, LAST)),
            dma((2, 3)), dma((2, 3)),
            dma((NX - 1,)), dma((NX - 1,)),
            dma((STEPS,)), dma((STEPS,)),
            dma((STEPS, NY - 1)), dma((STEPS, NY - 1)),
            dma((STEPS, 2)), dma((NX, 2, 2)),
            dma((NX - 1,)), dma((NX - 1,)),
            dma((NT - 1,)), dma((NT - 1,)),
        ],
        compiler_params=pltpu.CompilerParams(
            collective_id=0, has_side_effects=True, vmem_limit_bytes=56 << 20
        ),
    )(q, k, v, w, jnp.swapaxes(down[0], 0, 1), up, tenants, page_slots, lengths)


def solution(mesh):
    placed = (
        P("group", "tensor"),
        P("group", "tensor"),
        P("group", "tensor"),
        P("tensor", "group"),
        P("group", "tensor", None),
        P(None, None, "tensor"),
        P("group"),
        P(),
        P(),
    )
    return jax.shard_map(
        per_device, mesh=mesh, in_specs=placed, out_specs=P("group", "tensor"), check_vma=False
    )
```

time: 352 us -> 117 us (0.33)
  waiting for transfers between devices: 260 us -> 0 us
  Pallas kernels: 0 us -> 114 us
  matrix products: 29.5 us -> 0 us
  blocking collectives: 28.4 us -> 0 us
  between operations: 13.2 us -> 0.01 us
  starting transfers between devices: 6.85 us -> 0 us
  local copies, waits for them, and re-layouts: 6.58 us -> 1.87 us
  other arithmetic: 4.53 us -> 0 us
    all_gather x2 -> x0, waiting for transfers between devices: 151 us -> none  [the longest x1 148 us: per_device(): lax.all_gather(head_result, 'group', axis=0, tiled=True)]
    pallas_call x0 -> x1, Pallas kernels: none -> 114 us  [per_device(): pl.pallas_call(kernel, out_shape=jax.ShapeDtypeStruct((rows, WIDTH), BF16...]
    all_to_all x1 -> x0, waiting for transfers between devices: 102 us -> none  [per_device(): lax.all_to_all(projected, 'group', split_axis=0, concat_axis=1, tiled=True)]
    dot_general x7 -> x0, matrix products: 29.5 us -> none  [the longest x1 12.5 us: per_device(): jnp.dot(lax.all_gather(head_result, 'group', axis=0, tiled=True), output_...]
    psum x1 -> x0, blocking collectives: 28.4 us -> none  [per_device(): down_projected = lax.psum(shrunk_part.astype(jnp.bfloat16), 'tensor')]
    all_to_all x1 -> x0, starting transfers between devices: 6.58 us -> none  [per_device(): lax.all_to_all(projected, 'group', split_axis=0, concat_axis=1, tiled=True)]
    reduce_scatter x1 -> x0, waiting for transfers between devices: 6.49 us -> none  [per_device(): lax.psum_scatter(partial_value.astype(jnp.bfloat16), 'tensor', scatter_di...]
    all_to_all x1 -> x0, local copies, waits for them, and re-layouts: 4.7 us -> none  [per_device(): lax.all_to_all(projected, 'group', split_axis=0, concat_axis=1, tiled=True)]
  transfers between devices with their start and end apart: 4 -> 0, of which waited for: 4 -> 0; matrix products, arithmetic and copies ran while one was open for 5% -> 0% of each run, Pallas kernels for 0% -> 0%
where the time goes in v1:
time: 117 us; the launch traced here: 116 us
  Pallas kernels  114 us (97%)
  local copies, waits for them, and re-layouts  1.87 us (2%)
    pallas_call x1, Pallas kernels, per_device(): pl.pallas_call(kernel, out_shape=jax.ShapeDtypeStruct((rows, WIDTH), BF16...  114 us

profile of v1, /device:TPU:121, one launch (start us, length us, event | category | flops | bytes accessed | tf_op | source)
XLA Modules:
  0.0 115.8 jit_solution(10921849316347284865)
XLA Ops:
  0.0 114.0 %shard_map.91 = bf16[256,1024]{1,0:T(8,128)(2,1)} custom-call(bf16[256,1024]{1,0:T(8,128)(2,1)} %q_hbm.1, bf16[256,128]{1,0:T(8,128)(2,1)} %k_hbm.1, bf16[256,128]{1,0:T(8,128)(2,1)} %v_hbm.1, bf16[1024,256]{1,0:T(8,128)(2,1)} %w_hbm.1, bf16[64,1024]{1,0:T(8,128)(2,1)} %bitcast.3, bf16[32,64,1024]{2,1,0:T(8,128)(2,1)} %up_hbm.1, s32[2]{0:T(128)} %tenant_ref.1, ...), custom_call_target="tpu_custom_call" | custom-call | tf_op jit(solution)/shard_map/pallas_call | solution.py:390
  114.0 1.9 %copy.11 = bf16[256,1024]{1,0:T(8,128)(2,1)} copy(bf16[256,1024]{1,0:T(8,128)(2,1)} %shard_map.91) | data formatting | bytes 1048576

commit v2 on v1

v2 whole, which is shorter than its diff:
```python
import functools

import jax
import jax.numpy as jnp
from jax import lax
from jax.experimental import pallas as pl
from jax.experimental.pallas import tpu as pltpu
from jax.sharding import PartitionSpec as P

MESH = pl.DeviceIdType.MESH
HEADS = 8
DIM = 128
BLOCK = 128
NZ, NX, NY, NT = 8, 4, 4, 8
WIDTH = 1024
LAST = 7
GROUPS = ((0, 1), (1, 2), (3, 2), (5, 1), (6, 1), (7, 1))
ORDER = (
    "m0", "m1", "w4", "m2", "q0", "q1", "f0", "w5", "m3", "q2", "f1", "p6",
    "p7", "s0", "q3", "f2", "w6", "m4", "x0", "f3", "q4", "w7", "m5", "f4",
    "e0", "q5", "f5",
)
EXP2_SCALE = DIM ** (-0.5) * 1.4426950408889634
F32 = jnp.float32
BF16 = jnp.bfloat16


def matmul(a, b):
    return jnp.dot(a, b, preferred_element_type=F32)


def matmul_t(a, b):
    return lax.dot_general(a, b, (((1,), (1,)), ((), ())), preferred_element_type=F32)


def kernel(
    q_hbm, k_hbm, v_hbm, w_hbm, down_hbm, up_hbm, tenant_ref, slot_ref, length_ref,
    out_ref,
    qv, kv, vv, hbuf, slots, wbuf, pbuf, upv,
    kept, hsend, hrec, qsend, qrec, fsend, fin, acc,
    asend, arec, tsend, trec,
    lsem, wfs, wfr, wss, wrs, pfs, pfr, pss, prs, wps, wpr, hss, hrs, hps, hpr, sss, srs,
    hfs, hfr, qfs, qfr, fss, frs, axs, axr, ats, atr,
):
    g, t = lax.axis_index("group"), lax.axis_index("tensor")
    z, x = g // NX, g % NX
    y, c = t // 2, t % 2
    z_next = ((z + 1) % NZ) * NX + x
    z_prev = ((z + NZ - 1) % NZ) * NX + x
    sibling = (g, 2 * y + 1 - c)
    onward = (z_next * (1 - c) + z_prev * c, t)

    barrier = pltpu.get_barrier_semaphore()
    for peer in (z_next, z_prev):
        for core in range(2):
            pl.semaphore_signal(
                barrier, inc=1, device_id=(peer, 2 * y + core), device_id_type=MESH
            )

    def greet(d, carry):
        peer = (x * NT + t + d) % (NX * NT)
        pl.semaphore_signal(
            barrier, inc=1, device_id=(z * NX + peer // NT, peer % NT), device_id_type=MESH
        )
        return carry

    lax.fori_loop(1, NX * NT, greet, 0)
    pl.semaphore_wait(barrier, NX * NT + 3)

    def remote(src, dst, ssem, rsem, device):
        return pltpu.make_async_remote_copy(
            src_ref=src, dst_ref=dst, send_sem=ssem, recv_sem=rsem,
            device_id=device, device_id_type=MESH,
        )

    def place(k, core):
        off = (k + 1) // 2
        return (z + off * (NZ - 1 + 2 * core)) % NZ, ((k + 1) % 2 + core) % 2

    def w_first(core, s):
        half = s % 2 if core == 0 else 1 - s % 2
        return remote(
            w_hbm.at[:, half * 128 : half * 128 + 128], wbuf.at[s + 1, c],
            wfs.at[core, s], wfr.at[s, c], (z_next if core == 0 else z_prev, 2 * y + core),
        )

    def p_first(core, s):
        half = s % 2 if core == 0 else 1 - s % 2
        return remote(
            down_hbm.at[half * 32 : half * 32 + 32, :], pbuf.at[s + 1, c],
            pfs.at[core, s], pfr.at[s, c], (z_next if core == 0 else z_prev, 2 * y + core),
        )

    def w_copy(s):
        return remote(wbuf.at[s - 1], wbuf.at[s + 1], wss.at[s], wrs.at[s], onward)

    def p_copy(s):
        return remote(pbuf.at[s - 1], pbuf.at[s + 1], pss.at[s], prs.at[s], onward)

    for s in range(2):
        for make in (p_first, w_first):
            for core in range(2):
                make(core, s).start()

    def arrived(buf, fr, make, j):
        if j <= 2:
            for core in range(2):
                at = buf.at[j, core]
                remote(at, at, wss.at[0], fr.at[j - 1, core], onward).wait_recv()
        else:
            make(j - 1).wait_recv()
        if j + 1 < LAST:
            make(j + 1).start()

    w_arrived = functools.partial(arrived, wbuf, wfr, w_copy)
    p_arrived = functools.partial(arrived, pbuf, pfr, p_copy)

    def halves(ref, at):
        return ref.at[:, pl.ds(pl.multiple_of(at * 128, 128), 128)]

    w_pair = remote(halves(w_hbm, c), wbuf.at[0, c], wps.at[0], wpr.at[0], sibling)
    p_pair = remote(
        down_hbm.at[pl.ds(pl.multiple_of(c * 32, 32), 32), :], pbuf.at[0, c],
        wps.at[1], wpr.at[1], sibling,
    )
    q_in = pltpu.make_async_copy(q_hbm, qv, lsem.at[0])
    k_in = pltpu.make_async_copy(k_hbm, kv, lsem.at[1])
    v_in = pltpu.make_async_copy(v_hbm, vv, lsem.at[2])
    w_in = pltpu.make_async_copy(halves(w_hbm, 1 - c), wbuf.at[0, c], lsem.at[3])
    d_in = pltpu.make_async_copy(
        down_hbm.at[pl.ds(pl.multiple_of((1 - c) * 32, 32), 32), :], pbuf.at[0, c], lsem.at[4]
    )
    up_in = pltpu.make_async_copy(up_hbm, upv, lsem.at[5])
    for copy in (k_in, q_in, v_in, w_in, d_in, up_in):
        copy.start()

    tenant0, tenant1 = tenant_ref[0], tenant_ref[1]
    same = tenant0 == tenant1
    length0, length1 = length_ref[tenant0], length_ref[tenant1]
    slot0, slot1 = slot_ref[tenant0], slot_ref[tenant1]
    shift1 = jnp.where(same, BLOCK, 0)
    reach0 = jnp.where(same, length0, 0)

    rows8 = lax.broadcasted_iota(jnp.int32, (8, 128), 0)
    slots[x] = jnp.where(rows8 == 0, slot0, slot1).astype(F32)

    def slot_copy(d):
        return remote(
            slots.at[x], slots.at[x], sss.at[d - 1], srs.at[d - 1], (z * NX + (x + d) % NX, t)
        )

    def piece(core, tile, b):
        return hbuf.at[core, tile, b * BLOCK : (b + 1) * BLOCK, :]

    def h_copy(d, i):
        if i < 2:
            b, tile = i, x
        else:
            b, tile = d, (x + NX - 1) % NX if d == 0 else (x + 1) % NX
        to = (x + 1) % NX if d == 0 else (x + NX - 1) % NX
        at = piece(c, tile, b)
        return remote(at, at, hss.at[d, i], hrs.at[d, i], (z * NX + to, t))

    def h_pair(i, b):
        at = piece(c, (x + i) % NX, b)
        return remote(at, at, hps.at[i, b], hpr.at[i, b], sibling)

    k_in.wait()
    q_in.wait()
    v_in.wait()
    row = lax.broadcasted_iota(jnp.int32, (BLOCK, BLOCK), 0)
    col = lax.broadcasted_iota(jnp.int32, (BLOCK, BLOCK), 1)
    causal = col <= row
    masks = (
        [causal & (col < length0)],
        [col < reach0, causal & (col + shift1 < length1)],
    )
    for b in range(2):
        keys = [kv[j * BLOCK : (j + 1) * BLOCK, :] for j in range(b + 1)]
        values = [vv[j * BLOCK : (j + 1) * BLOCK, :] for j in range(b + 1)]
        for h in range(HEADS):
            query = qv[b * BLOCK : (b + 1) * BLOCK, h * DIM : (h + 1) * DIM]
            scores = [
                jnp.where(mask, matmul_t(query, key), -1e30)
                for mask, key in zip(masks[b], keys)
            ]
            peak = functools.reduce(
                jnp.maximum, [jnp.max(s, axis=1, keepdims=True) for s in scores]
            )
            expo = [jnp.exp2((s - peak) * EXP2_SCALE) for s in scores]
            total = functools.reduce(
                jnp.add, [jnp.sum(e, axis=1, keepdims=True) for e in expo]
            )
            inverse = 1.0 / total
            mixed = functools.reduce(
                jnp.add,
                [matmul((e * inverse).astype(BF16), value) for e, value in zip(expo, values)],
            )
            hbuf[c, x, b * BLOCK : (b + 1) * BLOCK, h * DIM : (h + 1) * DIM] = mixed.astype(BF16)
        for d in range(2):
            h_copy(d, b).start()
        h_pair(0, b).start()
    w_pair.start()
    p_pair.start()
    for d in range(1, NX):
        slot_copy(d).start()

    def h_arrived(d, i):
        h_copy(d, i).wait_recv()
        if (d, i) in ((0, 0), (1, 1)):
            h_copy(d, 2).start()
        at, b = ((3, i), (1, i))[d] if i < 2 else (2, d)
        h_pair(at, b).start()

    w_arrived(1)
    p_arrived(1)
    h_arrived(0, 0)
    h_arrived(1, 0)
    p_arrived(2)
    w_arrived(2)
    p_arrived(3)
    h_arrived(1, 1)
    h_arrived(0, 1)
    p_arrived(4)
    w_arrived(3)
    p_arrived(5)
    h_arrived(0, 2)
    h_arrived(1, 2)
    w_in.wait()
    d_in.wait()
    up_in.wait()
    w_pair.wait_recv()
    p_pair.wait_recv()
    for d in range(1, NX):
        slot_copy(d).wait_recv()
    for i in (0, 3, 1, 2):
        for b in range(2):
            h_pair(i, b).wait_recv()

    near = (y + 1 - 2 * (y % 2), NY - 1 - y)
    first = near[0] * (1 - c) + near[1] * c
    second = near[1] * (1 - c) + near[0] * c

    def set_of(n, at):
        return (x + (1 + 2 * c) * (at + n)) % NX

    def half_copy(n):
        k, count = GROUPS[n]
        return remote(
            hsend.at[k : k + count], hrec.at[k : k + count], hfs.at[n], hfr.at[n],
            (g, 2 * first + c),
        )

    def quarter_copy(n):
        k, count = GROUPS[n]
        return remote(
            qsend.at[k : k + count], qrec.at[k : k + count], qfs.at[n], qfr.at[n],
            (g, 2 * second + c),
        )

    def multiply(n):
        k, count = GROUPS[n]
        weights = [
            jnp.concatenate([wbuf[k + i, core] for i in range(count)], axis=1)
            for core in range(2)
        ]

        def rows(at, dst, i):
            at = set_of(n, at)
            value = matmul(hbuf[0, at], weights[0]) + matmul(hbuf[1, at], weights[1])
            for j in range(count):
                dst[k + j, i] = value[:, j * 128 : (j + 1) * 128].astype(BF16)

        rows(first, hsend, 0)
        rows((y + 2) % NY, hsend, 1)
        half_copy(n).start()
        rows(second, kept, 1)
        rows(y, kept, 0)

    def quarter(n):
        k, count = GROUPS[n]
        half_copy(n).wait_recv()
        for j in range(k, k + count):
            qsend[j] = (kept[j, 1].astype(F32) + hrec[j, 1].astype(F32)).astype(BF16)
        quarter_copy(n).start()

    def fin_copy(n):
        k, count = GROUPS[n]
        tile, half = place(k, c)
        dst = fin.at[x] if count == 2 else fin.at[x, pl.ds(half, 1)]
        return remote(
            fsend.at[k : k + count], dst, fss.at[n], frs.at[n, x, c],
            (z * NX + set_of(n, y), tile),
        )

    def stays(n):
        return (set_of(n, y) == x) & (place(GROUPS[n][0], c)[0] == t)

    def finish(n):
        k, count = GROUPS[n]
        quarter_copy(n).wait_recv()
        for j in range(k, k + count):
            value = (
                kept[j, 0].astype(F32) + hrec[j, 0].astype(F32) + qrec[j].astype(F32)
            ).astype(BF16)
            half = place(j, c)[1]
            fsend[k + half if count == 2 else k] = value

            @pl.when(stays(n))
            def _():
                fin[x, half] = value

        @pl.when(jnp.logical_not(stays(n)))
        def _():
            fin_copy(n).start()

    def shrink_copy(d):
        return remote(
            asend.at[(x + d) % NX], arec.at[d - 1], axs.at[d - 1], axr.at[d - 1],
            (z * NX + (x + d) % NX, t),
        )

    def tensor_copy(d):
        return remote(tsend, trec.at[d - 1], ats.at[d - 1], atr.at[d - 1], (g, (t + d) % NT))

    def shrink():
        pages = [pbuf[:, core].reshape(NZ * 32, WIDTH) for core in range(2)]
        lane = lax.broadcasted_iota(jnp.int32, (1, NZ * 32), 1)
        page = (place(lane // 32, c)[0] * NX + x).astype(F32)
        at = lax.broadcasted_iota(jnp.int32, (NZ * 32, 128), 0)
        at = at % 32 + 32 * place(at // 32, c)[1]
        to = lax.broadcasted_iota(jnp.int32, (NZ * 32, 128), 1)
        for i in range(NX):
            total = jnp.zeros((BLOCK, 128), F32)
            value = matmul_t(hbuf[0, i], pages[0]) + matmul_t(hbuf[1, i], pages[1])
            for b in range(2):
                slot = jnp.concatenate([slots[i, b : b + 1, :]] * (NZ * 32 // 128), axis=1)
                rows = jnp.where(slot == page, value[b * BLOCK : (b + 1) * BLOCK, :], 0.0)
                total = total + matmul(rows.astype(BF16), (to == at + 64 * b).astype(BF16))
            asend[i] = total.astype(BF16)
        for d in range(1, NX):
            shrink_copy(d).start()

    def shrink_x():
        total = asend[x].astype(F32)
        for d in range(1, NX):
            shrink_copy(d).wait_recv()
            total = total + arec[d - 1].astype(F32)
        tsend[...] = total.astype(BF16)
        for d in range(1, NT):
            tensor_copy(d).start()

    def expand():
        total = tsend[...].astype(F32)
        for d in range(1, NT):
            tensor_copy(d).wait_recv()
            total = total + trec[d - 1].astype(F32)
        shrunk = total.astype(BF16)
        lane = lax.broadcasted_iota(jnp.int32, (BLOCK, 128), 1)
        for b, slot in enumerate((slot0, slot1)):
            acc[b * BLOCK : (b + 1) * BLOCK, :] = matmul(
                jnp.where(lane // 64 == b, shrunk, jnp.zeros_like(shrunk)),
                jnp.concatenate([upv[slot], upv[slot]], axis=0),
            )

    stages = {
        "m": multiply, "q": quarter, "f": finish, "w": w_arrived, "p": p_arrived,
        "s": lambda _: shrink(), "x": lambda _: shrink_x(), "e": lambda _: expand(),
    }
    for stage in ORDER:
        stages[stage[0]](int(stage[1]))

    for s in range(2):
        for core in range(2):
            w_first(core, s).wait_send()
            p_first(core, s).wait_send()

    def sent(s, carry):
        w_copy(s).wait_send()
        p_copy(s).wait_send()
        return carry

    lax.fori_loop(2, LAST, sent, 0)
    w_pair.wait_send()
    p_pair.wait_send()
    for d in range(2):
        for i in range(3):
            h_copy(d, i).wait_send()
    for i in range(NX):
        for b in range(2):
            h_pair(i, b).wait_send()
    for d in range(1, NX):
        slot_copy(d).wait_send()
        shrink_copy(d).wait_send()
    for d in range(1, NT):
        tensor_copy(d).wait_send()
    for n in range(len(GROUPS)):
        half_copy(n).wait_send()
        quarter_copy(n).wait_send()

        @pl.when(jnp.logical_not(stays(n)))
        def _():
            fin_copy(n).wait_send()

    for n, (k, count) in enumerate(GROUPS):
        for core in range(2):
            tile, half = place(k, core)

            @pl.when(tile == t)
            def _():
                for i in range(NX):

                    @pl.when(jnp.logical_not(stays(n) & (x == i) & (c == core)))
                    def _():
                        at = fin.at[i, pl.ds(0, count)]
                        remote(at, at, fss.at[0], frs.at[n, i, core], sibling).wait_recv()

    position = lax.broadcasted_iota(jnp.int32, (BLOCK, 128), 0)
    valid = (position < length0, position + shift1 < length1)
    for b in range(2):
        for i in range(NX):
            for half in range(2):
                cols = slice(i * 256 + half * 128, i * 256 + half * 128 + 128)
                base = fin[i, half, b * BLOCK : (b + 1) * BLOCK, :].astype(F32)
                value = base + acc[b * BLOCK : (b + 1) * BLOCK, cols]
                out_ref[b * BLOCK : (b + 1) * BLOCK, cols] = jnp.where(
                    valid[b], value, 0.0
                ).astype(BF16)


def per_device(q, k, v, w, down, up, tenants, page_slots, lengths):
    dma = pltpu.SemaphoreType.DMA
    anywhere = pl.BlockSpec(memory_space=pl.ANY)
    scalars = pl.BlockSpec(memory_space=pltpu.SMEM)
    rows = 2 * BLOCK
    groups = len(GROUPS)
    return pl.pallas_call(
        kernel,
        out_shape=jax.ShapeDtypeStruct((rows, WIDTH), BF16),
        in_specs=[anywhere] * 6 + [scalars] * 3,
        out_specs=pl.BlockSpec(memory_space=pltpu.VMEM),
        scratch_shapes=[
            pltpu.VMEM((rows, WIDTH), BF16),
            pltpu.VMEM((rows, DIM), BF16),
            pltpu.VMEM((rows, DIM), BF16),
            pltpu.VMEM((2, NX, rows, WIDTH), BF16),
            pltpu.VMEM((NX, 8, 128), F32),
            pltpu.VMEM((NZ, 2, WIDTH, 128), BF16),
            pltpu.VMEM((NZ, 2, 32, WIDTH), BF16),
            pltpu.VMEM((32, 64, WIDTH), BF16),
            pltpu.VMEM((NZ, 2, rows, 128), BF16),
            pltpu.VMEM((NZ, 2, rows, 128), BF16),
            pltpu.VMEM((NZ, 2, rows, 128), BF16),
            pltpu.VMEM((NZ, rows, 128), BF16),
            pltpu.VMEM((NZ, rows, 128), BF16),
            pltpu.VMEM((NZ, rows, 128), BF16),
            pltpu.VMEM((NX, 2, rows, 128), BF16),
            pltpu.VMEM((rows, WIDTH), F32),
            pltpu.VMEM((NX, BLOCK, 128), BF16),
            pltpu.VMEM((NX - 1, BLOCK, 128), BF16),
            pltpu.VMEM((BLOCK, 128), BF16),
            pltpu.VMEM((NT - 1, BLOCK, 128), BF16),
            dma((6,)),
            dma((2, 2)), dma((2, 2)), dma((LAST,)), dma((LAST,)),
            dma((2, 2)), dma((2, 2)), dma((LAST,)), dma((LAST,)),
            dma((2,)), dma((2,)),
            dma((2, 3)), dma((2, 3)), dma((NX, 2)), dma((NX, 2)),
            dma((NX - 1,)), dma((NX - 1,)),
            dma((groups,)), dma((groups,)), dma((groups,)), dma((groups,)),
            dma((groups,)), dma((groups, NX, 2)),
            dma((NX - 1,)), dma((NX - 1,)),
            dma((NT - 1,)), dma((NT - 1,)),
        ],
        compiler_params=pltpu.CompilerParams(
            collective_id=0, has_side_effects=True, vmem_limit_bytes=56 << 20
        ),
    )(q, k, v, w, jnp.swapaxes(down[0], 0, 1), up, tenants, page_slots, lengths)


def solution(mesh):
    placed = (
        P("group", "tensor"),
        P("group", "tensor"),
        P("group", "tensor"),
        P("tensor", "group"),
        P("group", "tensor", None),
        P(None, None, "tensor"),
        P("group"),
        P(),
        P(),
    )
    return jax.shard_map(
        per_device, mesh=mesh, in_specs=placed, out_specs=P("group", "tensor"), check_vma=False
    )
```

time: 117 us -> 89.9 us (0.77)
  Pallas kernels: 114 us -> 87.9 us
    pallas_call x1, Pallas kernels: 114 us -> 87.9 us  [per_device(): pl.pallas_call(kernel, out_shape=jax.ShapeDtypeStruct((rows, WIDTH), BF16...]
where the time goes in v2:
time: 89.9 us; the launch traced here: 89.7 us
  Pallas kernels  87.9 us (98%)
  local copies, waits for them, and re-layouts  1.87 us (2%)
    pallas_call x1, Pallas kernels, per_device(): pl.pallas_call(kernel, out_shape=jax.ShapeDtypeStruct((rows, WIDTH), BF16...  87.9 us
    unnamed x1, local copies, waits for them, and re-layouts  1.87 us

profile of v2, /device:TPU:121, one launch (start us, length us, event | category | flops | bytes accessed | tf_op | source)
XLA Modules:
  0.0 89.7 jit_solution(12037998620583653921)
XLA Ops:
  0.0 87.9 %shard_map.91 = bf16[256,1024]{1,0:T(8,128)(2,1)} custom-call(bf16[256,1024]{1,0:T(8,128)(2,1)} %q_hbm.1, bf16[256,128]{1,0:T(8,128)(2,1)} %k_hbm.1, bf16[256,128]{1,0:T(8,128)(2,1)} %v_hbm.1, bf16[1024,256]{1,0:T(8,128)(2,1)} %w_hbm.1, bf16[64,1024]{1,0:T(8,128)(2,1)} %bitcast.3, bf16[32,64,1024]{2,1,0:T(8,128)(2,1)} %up_hbm.1, s32[2]{0:T(128)} %tenant_ref.1, ...), custom_call_target="tpu_custom_call" | custom-call | tf_op jit(solution)/shard_map/pallas_call | solution.py:437
  87.9 1.9 %copy.11 = bf16[256,1024]{1,0:T(8,128)(2,1)} copy(bf16[256,1024]{1,0:T(8,128)(2,1)} %shard_map.91) | data formatting | bytes 1048576

commit v3 on v2

--- a/solution.py
+++ b/solution.py
@@ -16,9 +16,9 @@
 LAST = 7
 GROUPS = ((0, 1), (1, 2), (3, 2), (5, 1), (6, 1), (7, 1))
 ORDER = (
-    "m0", "m1", "w4", "m2", "q0", "q1", "f0", "w5", "m3", "q2", "f1", "p6",
-    "p7", "s0", "q3", "f2", "w6", "m4", "x0", "f3", "q4", "w7", "m5", "f4",
-    "e0", "q5", "f5",
+    "m0", "m1", "q0", "w4", "m2", "q1", "f0", "w5", "m3", "q2", "f1", "p6",
+    "p7", "w6", "m4", "q3", "f2", "f3", "q4", "s0", "w7", "m5", "f4", "x0",
+    "q5", "e0", "f5",
 )
 EXP2_SCALE = DIM ** (-0.5) * 1.4426950408889634
 F32 = jnp.float32

time: 89.9 us -> 88.7 us (0.987)
  Pallas kernels: 87.9 us -> 85.8 us
    pallas_call x1, Pallas kernels: 87.9 us -> 85.8 us  [per_device(): pl.pallas_call(kernel, out_shape=jax.ShapeDtypeStruct((rows, WIDTH), BF16...]
where the time goes in v3:
time: 88.7 us; the launch traced here: 87.7 us
  Pallas kernels  85.8 us (97%)
  local copies, waits for them, and re-layouts  1.87 us (2%)
    pallas_call x1, Pallas kernels, per_device(): pl.pallas_call(kernel, out_shape=jax.ShapeDtypeStruct((rows, WIDTH), BF16...  85.8 us
    unnamed x1, local copies, waits for them, and re-layouts  1.87 us

profile of v3, /device:TPU:121, one launch (start us, length us, event | category | flops | bytes accessed | tf_op | source)
XLA Modules:
  0.0 87.7 jit_solution(9704811326264283172)
XLA Ops:
  0.0 85.8 %shard_map.91 = bf16[256,1024]{1,0:T(8,128)(2,1)} custom-call(bf16[256,1024]{1,0:T(8,128)(2,1)} %q_hbm.1, bf16[256,128]{1,0:T(8,128)(2,1)} %k_hbm.1, bf16[256,128]{1,0:T(8,128)(2,1)} %v_hbm.1, bf16[1024,256]{1,0:T(8,128)(2,1)} %w_hbm.1, bf16[64,1024]{1,0:T(8,128)(2,1)} %bitcast.3, bf16[32,64,1024]{2,1,0:T(8,128)(2,1)} %up_hbm.1, s32[2]{0:T(128)} %tenant_ref.1, ...), custom_call_target="tpu_custom_call" | custom-call | tf_op jit(solution)/shard_map/pallas_call | solution.py:437
  85.9 1.9 %copy.11 = bf16[256,1024]{1,0:T(8,128)(2,1)} copy(bf16[256,1024]{1,0:T(8,128)(2,1)} %shard_map.91) | data formatting | bytes 1048576

commit v4 on v3

--- a/solution.py
+++ b/solution.py
@@ -50,6 +50,12 @@
     sibling = (g, 2 * y + 1 - c)
     onward = (z_next * (1 - c) + z_prev * c, t)
 
+    q_in = pltpu.make_async_copy(q_hbm, qv, lsem.at[0])
+    k_in = pltpu.make_async_copy(k_hbm, kv, lsem.at[1])
+    v_in = pltpu.make_async_copy(v_hbm, vv, lsem.at[2])
+    for copy in (k_in, q_in, v_in):
+        copy.start()
+
     barrier = pltpu.get_barrier_semaphore()
     for peer in (z_next, z_prev):
         for core in range(2):
@@ -123,15 +129,12 @@
         down_hbm.at[pl.ds(pl.multiple_of(c * 32, 32), 32), :], pbuf.at[0, c],
         wps.at[1], wpr.at[1], sibling,
     )
-    q_in = pltpu.make_async_copy(q_hbm, qv, lsem.at[0])
-    k_in = pltpu.make_async_copy(k_hbm, kv, lsem.at[1])
-    v_in = pltpu.make_async_copy(v_hbm, vv, lsem.at[2])
     w_in = pltpu.make_async_copy(halves(w_hbm, 1 - c), wbuf.at[0, c], lsem.at[3])
     d_in = pltpu.make_async_copy(
         down_hbm.at[pl.ds(pl.multiple_of((1 - c) * 32, 32), 32), :], pbuf.at[0, c], lsem.at[4]
     )
     up_in = pltpu.make_async_copy(up_hbm, upv, lsem.at[5])
-    for copy in (k_in, q_in, v_in, w_in, d_in, up_in):
+    for copy in (w_in, d_in, up_in):
         copy.start()
 
     tenant0, tenant1 = tenant_ref[0], tenant_ref[1]

time: 88.7 us -> 88.7 us (level)
  no operation moved by 1% of the time
where the time goes in v4:
time: 88.7 us; the launch traced here: 87.7 us
  Pallas kernels  85.8 us (97%)
  local copies, waits for them, and re-layouts  1.87 us (2%)
    pallas_call x1, Pallas kernels, per_device(): pl.pallas_call(kernel, out_shape=jax.ShapeDtypeStruct((rows, WIDTH), BF16...  85.8 us
    unnamed x1, local copies, waits for them, and re-layouts  1.87 us

profile of v4, /device:TPU:121, one launch (start us, length us, event | category | flops | bytes accessed | tf_op | source)
XLA Modules:
  0.0 87.7 jit_solution(891012423701273382)
XLA Ops:
  0.0 85.8 %shard_map.91 = bf16[256,1024]{1,0:T(8,128)(2,1)} custom-call(bf16[256,1024]{1,0:T(8,128)(2,1)} %q_hbm.1, bf16[256,128]{1,0:T(8,128)(2,1)} %k_hbm.1, bf16[256,128]{1,0:T(8,128)(2,1)} %v_hbm.1, bf16[1024,256]{1,0:T(8,128)(2,1)} %w_hbm.1, bf16[64,1024]{1,0:T(8,128)(2,1)} %bitcast.3, bf16[32,64,1024]{2,1,0:T(8,128)(2,1)} %up_hbm.1, s32[2]{0:T(128)} %tenant_ref.1, ...), custom_call_target="tpu_custom_call" | custom-call | tf_op jit(solution)/shard_map/pallas_call | solution.py:440
  85.9 1.9 %copy.11 = bf16[256,1024]{1,0:T(8,128)(2,1)} copy(bf16[256,1024]{1,0:T(8,128)(2,1)} %shard_map.91) | data formatting | bytes 1048576
